TPU v7x, 32 devices: a whole 2x2x4 slice. The times are simulated.
32 devices in a mesh: dp: 4 (over z), mp: 8 (over y, x, core).
Axes of the slice: x: 2, y: 2, z: 4, core: 2. Of those that a mesh axis runs over, the one named last changes fastest.
Arguments:
- guess_vectors: bfloat16 [128, 16, 4096], P(('dp', 'mp')), may hold values from -6 to 6
- preceding_symbol_vector: bfloat16 [128, 4096], P(('dp', 'mp')), may hold values from -6 to 6
- earlier_memory_matrix: float32 [128, 64, 64, 64], P('dp', 'mp'), may hold values from -4 to 4
- lag_blend_factor: float32 [4096], replicated, may hold values from 0 to 1
- constant_lag_blends: float32 [5, 4096], replicated, may hold values from 0 to 1
- blending_lower_matrix: bfloat16 [4096, 160], replicated, may hold values from -0.09375 to 0.09375
- blending_raise_matrix: bfloat16 [5, 32, 4096], replicated, may hold values from -1 to 1
- constant_fading: float32 [4096], P('mp'), may hold values from -6 to -1
- fading_lower_matrix: bfloat16 [4096, 64], replicated, may hold values from -0.09375 to 0.09375
- fading_raise_matrix: bfloat16 [64, 4096], P(None, 'mp'), may hold values from -1 to 1
- diagonal_boost: float32 [64, 64], P('mp'), may hold values from -3 to 3
- acceptor_matrix: bfloat16 [4096, 4096], P('dp', 'mp'), may hold values from -0.09375 to 0.09375
- lookup_matrix: bfloat16 [4096, 4096], P('dp', 'mp'), may hold values from -0.09375 to 0.09375
- payload_matrix: bfloat16 [4096, 4096], P('dp', 'mp'), may hold values from -0.09375 to 0.09375
- gating_matrix: bfloat16 [4096, 4096], P('dp', 'mp'), may hold values from -0.09375 to 0.09375
- emission_matrix: bfloat16 [4096, 4096], P('mp', 'dp'), may hold values from -0.09375 to 0.09375
- groupwise_scaling_factor: float32 [4096], P('mp'), may hold values from 0.1 to 1.9
- groupwise_scaling_offset: float32 [4096], P('mp'), may hold values from -3 to 3
- usable_guess_amount: int32 [128], replicated, may hold values from 1 to 16, as said below
- approved_guesses: int32 [128], replicated, may hold values from 0 to 16, as said below
- destination_slot: int32 [128], replicated, may hold values from 0 to 127, as said below
Outputs:
- layer_out: bfloat16 [128, 16, 4096], P(('dp', 'mp'))
- next_state: float32 [128, 64, 64, 64], P('dp', 'mp')
- next_edge: bfloat16 [128, 4096], P('dp', 'mp')
Inputs may be any that keep to these rules, and one draw needn't show every extreme that they name: `usable_guess_amount`: some request has all 16 draft tokens valid. approved_guesses[b] <= usable_guess_amount[b]; some request accepts all 16. destination_slot is a permutation of the requests. Of the 32 requests of one aligned block, at most 16 have owner slots in one aligned block of 32 slots, and some pair of blocks reaches 16.
All inputs are finite; a program needn't handle non-finite values.
Results may differ from a plain program's by a relative error of at most 0.007.
Values may be sent and summed in bfloat16 or wider, within the bound.
A program may use at most 256 MiB of HBM per device.

v0:
```python
import jax
import jax.numpy as jnp
from jax import lax
from jax.sharding import PartitionSpec as P

GROUP_DIMENSION = 64
norm_eps = 0.00064


def token_mixes(
    guess_vectors,
    edges,
    lag_blend_factor,
    constant_lag_blends,
    blending_lower_matrix,
    blending_raise_matrix,
):
    previous = jnp.concatenate([edges[:, None, :], guess_vectors[:, :-1, :]], axis=1)
    width = guess_vectors.shape[-1]
    current_input = guess_vectors.reshape(-1, width).astype(jnp.float32)
    shift_difference = previous.reshape(-1, width).astype(jnp.float32) - current_input
    shift_blended = (current_input + shift_difference * lag_blend_factor).astype(jnp.bfloat16)
    mixing_inner_all = jnp.tanh(
        jnp.dot(shift_blended, blending_lower_matrix, preferred_element_type=jnp.float32)
    ).astype(jnp.bfloat16)
    mixing_inner_width = blending_raise_matrix.shape[1]
    shift_mixed_rows = []
    for mix_component in range(5):
        mixing_inner_part = jnp.dot(
            mixing_inner_all[
                :, mix_component * mixing_inner_width : (mix_component + 1) * mixing_inner_width
            ],
            blending_raise_matrix[mix_component],
            preferred_element_type=jnp.float32,
        )
        shift_mixed_rows.append(
            (
                current_input
                + shift_difference * (constant_lag_blends[mix_component] + mixing_inner_part)
            ).astype(jnp.bfloat16)
        )
    return shift_mixed_rows


def wkv_blocks(
    acceptor_vectors,
    lookup_vectors,
    payload_vectors,
    logarithmic_fading_entries,
    diagonal_boost,
    starting_memory,
    approved_guesses,
):
    draft = acceptor_vectors.shape[1]
    cumulative = jnp.cumsum(logarithmic_fading_entries, axis=1)
    starts = jnp.concatenate(
        [jnp.zeros_like(logarithmic_fading_entries[:, :1]), cumulative], axis=1
    )
    before = starts[:, :draft]
    from_start = jnp.einsum(
        "bthi,bhij->bthj",
        acceptor_vectors * jnp.exp(before),
        starting_memory,
        precision=lax.Precision.HIGHEST,
    )
    later = jnp.arange(draft)[:, None] > jnp.arange(draft)[None, :]
    exponent = before[:, :, None] - cumulative[:, None, :]
    exponent = jnp.where(later[None, :, :, None, None], exponent, -1e30)
    scores = jnp.sum(
        acceptor_vectors[:, :, None] * lookup_vectors[:, None, :] * jnp.exp(exponent), axis=-1
    )
    inner = jnp.einsum("btsh,bshj->bthj", scores, payload_vectors, precision=lax.Precision.HIGHEST)
    diagonal_boost_contribution = (
        jnp.sum(acceptor_vectors * diagonal_boost * lookup_vectors, axis=-1, keepdims=True)
        * payload_vectors
    )
    outputs = from_start + inner + diagonal_boost_contribution
    at_accept = jnp.take_along_axis(starts, approved_guesses[:, None, None, None], axis=1)[:, 0]
    used = jnp.arange(draft)[None, :] < approved_guesses[:, None]
    coef_exp = jnp.where(used[:, :, None, None], at_accept[:, None] - cumulative, -1e30)
    weighted = jnp.exp(coef_exp) * lookup_vectors
    picked = jnp.exp(at_accept)[..., None] * starting_memory + jnp.einsum(
        "bshi,bshj->bhij", weighted, payload_vectors, precision=lax.Precision.HIGHEST
    )
    return (outputs, picked)


def gated_norm(outputs, gate_raw, gain, bias):
    centre = jnp.mean(outputs, axis=-1, keepdims=True)
    spread = outputs - centre
    variance = jnp.mean(spread * spread, axis=-1, keepdims=True)
    normed = (spread * lax.rsqrt(variance + norm_eps)).reshape(outputs.shape[0], -1)
    return ((normed * gain + bias) * jax.nn.silu(gate_raw)).astype(jnp.bfloat16)


def on_device(
    guess_vectors,
    preceding_symbol_vector,
    earlier_memory_matrix,
    lag_blend_factor,
    constant_lag_blends,
    blending_lower_matrix,
    blending_raise_matrix,
    constant_fading,
    fading_lower_matrix,
    fading_raise_matrix,
    diagonal_boost,
    acceptor_matrix,
    lookup_matrix,
    payload_matrix,
    gating_matrix,
    emission_matrix,
    groupwise_scaling_factor,
    groupwise_scaling_offset,
    usable_guess_amount,
    approved_guesses,
    destination_slot,
):
    own_reqs, draft, width = guess_vectors.shape
    group_count = lax.axis_size("mp")
    row_groups = lax.axis_size("dp")
    row_reqs = own_reqs * group_count
    row_index = lax.axis_index("dp")
    group_index = lax.axis_index("mp")
    local_width = acceptor_matrix.shape[1]
    local_heads = local_width // GROUP_DIMENSION
    gathered, edges_all = (
        lax.all_gather(guess_vectors, "mp", axis=0, tiled=True),
        lax.all_gather(preceding_symbol_vector, "mp", axis=0, tiled=True),
    )
    shift_mixed_rows = token_mixes(
        gathered,
        edges_all,
        lag_blend_factor,
        constant_lag_blends,
        blending_lower_matrix,
        blending_raise_matrix,
    )
    token_rows = row_reqs * draft
    sources = (shift_mixed_rows[3], shift_mixed_rows[1], shift_mixed_rows[2], shift_mixed_rows[4])
    pieces = (
        lax.all_gather(acceptor_matrix, "dp", axis=0, tiled=True),
        lax.all_gather(lookup_matrix, "dp", axis=0, tiled=True),
        lax.all_gather(payload_matrix, "dp", axis=0, tiled=True),
        lax.all_gather(gating_matrix, "dp", axis=0, tiled=True),
    )
    acceptor_vectors, lookup_vectors, payload_vectors, gate_raw = tuple(
        (
            jnp.dot(source_rows, piece, preferred_element_type=jnp.float32)
            for source_rows, piece in zip(sources, pieces)
        )
    )
    decay_inner_rows = jnp.tanh(
        jnp.dot(shift_mixed_rows[0], fading_lower_matrix, preferred_element_type=jnp.float32)
    ).astype(jnp.bfloat16)
    logarithmic_fading_entries = -jnp.exp(
        constant_fading
        + jnp.dot(decay_inner_rows, fading_raise_matrix, preferred_element_type=jnp.float32)
    )

    def to_heads(values):
        return values.reshape(row_reqs, draft, local_heads, GROUP_DIMENSION)

    row_accepted = lax.dynamic_slice_in_dim(approved_guesses, row_index * row_reqs, row_reqs)
    outputs, picked = wkv_blocks(
        to_heads(acceptor_vectors),
        to_heads(lookup_vectors),
        to_heads(payload_vectors),
        to_heads(logarithmic_fading_entries),
        diagonal_boost,
        earlier_memory_matrix,
        row_accepted,
    )
    hidden = gated_norm(
        outputs.reshape(token_rows, local_heads, GROUP_DIMENSION),
        gate_raw,
        groupwise_scaling_factor,
        groupwise_scaling_offset,
    )
    out_cols = lax.all_gather(emission_matrix, "dp", axis=1, tiled=True)
    attended = lax.psum_scatter(
        jnp.dot(hidden, out_cols, preferred_element_type=jnp.float32).astype(jnp.bfloat16),
        "mp",
        scatter_dimension=0,
        tiled=True,
    ).astype(jnp.float32)
    own_start = (row_index * group_count + group_index) * own_reqs
    own_lengths = lax.dynamic_slice_in_dim(usable_guess_amount, own_start, own_reqs)
    valid_mask = jnp.arange(draft, dtype=jnp.int32)[None, :] < own_lengths[:, None]
    layer_out = (
        guess_vectors.astype(jnp.float32)
        + jnp.where(
            valid_mask[..., None],
            attended.reshape(own_reqs, draft, width),
            jnp.zeros((), jnp.float32),
        )
    ).astype(jnp.bfloat16)
    edge_rows = jnp.concatenate([edges_all[:, None, :], gathered], axis=1)
    edge_cols = lax.dynamic_slice_in_dim(edge_rows, group_index * local_width, local_width, 2)
    chosen = jnp.take_along_axis(edge_cols, row_accepted[:, None, None], axis=1)[:, 0]
    capacity = 2 * row_reqs // row_groups
    target_rows = (destination_slot // row_reqs).reshape(row_groups, row_reqs)
    onehot = (
        target_rows[:, :, None] == jnp.arange(row_groups, dtype=jnp.int32)[None, None, :]
    ).astype(jnp.int32)
    earlier = jnp.cumsum(onehot, axis=1) - onehot
    ranks = jnp.sum(earlier * onehot, axis=-1)
    my_targets = lax.dynamic_index_in_dim(target_rows, row_index, 0, keepdims=False)
    my_ranks = lax.dynamic_index_in_dim(ranks, row_index, 0, keepdims=False)
    selected = (
        my_targets[:, None, None] == jnp.arange(row_groups, dtype=jnp.int32)[None, :, None]
    ) & (my_ranks[:, None, None] == jnp.arange(capacity, dtype=jnp.int32)[None, None, :])
    source_index = jnp.sum(
        selected.astype(jnp.int32) * jnp.arange(row_reqs, dtype=jnp.int32)[:, None, None], axis=0
    )
    filled = jnp.any(selected, axis=0)
    send_state = jnp.where(
        filled[..., None, None, None], picked[source_index], jnp.zeros((), jnp.float32)
    )
    send_edge = jnp.where(
        filled[..., None], chosen[source_index].astype(jnp.float32), jnp.zeros((), jnp.float32)
    )
    recv_state, recv_edge = (
        lax.all_to_all(
            send_state.astype(jnp.bfloat16), "dp", split_axis=0, concat_axis=0, tiled=True
        ).astype(send_state.dtype),
        lax.all_to_all(
            send_edge.astype(jnp.bfloat16), "dp", split_axis=0, concat_axis=0, tiled=True
        ).astype(send_edge.dtype),
    )
    wanted = row_index * row_reqs + jnp.arange(row_reqs, dtype=jnp.int32)
    total_reqs = destination_slot.shape[0]
    matches = (destination_slot[None, :] == wanted[:, None]).astype(jnp.int32)
    which = jnp.sum(matches * jnp.arange(total_reqs, dtype=jnp.int32)[None, :], axis=1)
    flat_index = which // row_reqs * capacity + ranks.reshape(-1)[which]
    next_state = recv_state.reshape(
        row_groups * capacity, local_heads, GROUP_DIMENSION, GROUP_DIMENSION
    )[flat_index]
    next_edge = recv_edge.reshape(row_groups * capacity, local_width)[flat_index].astype(
        jnp.bfloat16
    )
    return (layer_out, next_state, next_edge)


def solution(mesh):
    in_specs = (
        P(("dp", "mp"), None, None),
        P(("dp", "mp"), None),
        P("dp", "mp", None, None),
        P(),
        P(),
        P(),
        P(),
        P("mp"),
        P(),
        P(None, "mp"),
        P("mp", None),
        P("dp", "mp"),
        P("dp", "mp"),
        P("dp", "mp"),
        P("dp", "mp"),
        P("mp", "dp"),
        P("mp"),
        P("mp"),
        P(),
        P(),
        P(),
    )
    out_specs = (P(("dp", "mp"), None, None), P("dp", "mp", None, None), P("dp", "mp"))
    return jax.shard_map(
        on_device, mesh=mesh, in_specs=in_specs, out_specs=out_specs, check_vma=False
    )
```

profile of v0, /device:TPU:0, one launch (start us, length us, event | category | flops | bytes accessed | tf_op | source)
XLA Modules:
  0.0 585.9 jit_solution(18396825524794450216)
XLA Ops:
  7.3 0.7 all-gather.8.cloned.1.call-update
  8.0 0.7 all-gather.12.cloned.1.call-update
  8.8 0.7 all-gather.14.cloned.1.call-update
  9.5 0.5 all-gather.10.cloned.1.call-update
  10.1 0.5 all-gather.16.cloned.1.call-update
  10.7 0.5 all-gather.18.cloned.1.call-update
  11.6 0.2 select_reduce_fusion
  11.9 0.1 fusion.58
  12.1 0.2 and_reduce_fusion
  12.2 10.8 %all-gather = bf16[8,4,4096]{2,1,0:T(4,128)(2,1)S(1)} all-gather(bf16[1,4,4096]{2,1,0:T(4,128)(2,1)S(1)} %bitcast.122), channel_id=1, replica_groups=mesh['dp'=4,'mp'=8] {'mp'}, dimensions={0}, use_global_device_ids=true | all-gather | bytes 294912 | tf_op jit(solution)/shard_map/all_gather | solution.py:129
  23.1 0.5 copy.66
  23.9 25.6 %all-gather.8.cloned.1.call-done = bf16[32,16,4096]{2,1,0:T(8,128)(2,1)} async-done(((bf16[4,16,4096]{2,1,0:T(8,128)(2,1)}), bf16[32,16,4096]{2,1,0:T(8,128)(2,1)}) %all-gather.8.cloned.1.call-update) | async-done | bytes 4194320 | tf_op jit(solution)/shard_map/all_gather | solution.py:128
  49.4 3.7 pad_maximum_fusion
  53.1 1.9 copy-done.7
  55.1 2.0 fusion.28
  57.1 74.7 %all-gather.12.cloned.1.call-done = bf16[4096,512]{1,0:T(8,128)(2,1)} async-done(((bf16[1024,512]{1,0:T(8,128)(2,1)}), bf16[4096,512]{1,0:T(8,128)(2,1)}) %all-gather.12.cloned.1.call-update) | async-done | bytes 4194320 | tf_op jit(solution)/shard_map/all_gather | solution.py:144
  131.8 8.5 %fusion.23 = f32[512,512]{1,0:T(8,128)S(1)} fusion(bf16[4096,512]{1,0:T(8,128)(2,1)} %all-gather.12.cloned.1.call-done, bf16[512,4096]{1,0:T(8,128)(2,1)} %bitcast.105, bf16[512,4096]{1,0:T(8,128)(2,1)} %bitcast.112, f32[4096]{0:T(1024)S(1)} %bitcast.127, bf16[5,32,4096]{2,1,0:T(8,128)(2,1)} %param.27, bf16[512,160]{0,1:T(8,128)(2,1)S(1)} %fusion.28), kind=kOutput, calls=%fused_computation.48 | convolution fusion | flops 2296381440 | bytes 13942784 | tf_op jit(solution)/shard_map/dot_general | solution.py:149
  140.3 1.8 reshape.356
  142.2 70.5 %all-gather.14.cloned.1.call-done = bf16[4096,512]{1,0:T(8,128)(2,1)} async-done(((bf16[1024,512]{1,0:T(8,128)(2,1)}), bf16[4096,512]{1,0:T(8,128)(2,1)}) %all-gather.14.cloned.1.call-update) | async-done | bytes 4194320 | tf_op jit(solution)/shard_map/all_gather | solution.py:143
  212.7 8.6 %fusion.22 = f32[512,512]{1,0:T(8,128)S(1)} fusion(bf16[4096,512]{1,0:T(8,128)(2,1)} %all-gather.14.cloned.1.call-done, bf16[512,4096]{1,0:T(8,128)(2,1)} %bitcast.106, bf16[512,4096]{1,0:T(8,128)(2,1)} %bitcast.113, f32[4096]{0:T(1024)S(1)} %bitcast.126, bf16[5,32,4096]{2,1,0:T(8,128)(2,1)} %param.27, bf16[512,160]{0,1:T(8,128)(2,1)S(1)} %fusion.28), kind=kOutput, calls=%fused_computation.47 | convolution fusion | flops 2296381440 | bytes 13942784 | tf_op jit(solution)/shard_map/dot_general | solution.py:149
  221.3 1.8 mul.159
  223.1 6.9 %fusion.32 = bf16[512,64]{0,1:T(8,128)(2,1)S(1)} fusion(bf16[4096,64]{0,1:T(8,128)(2,1)S(1)} %copy-done.19, bf16[512,4096]{1,0:T(8,128)(2,1)} %bitcast.107, bf16[512,4096]{1,0:T(8,128)(2,1)} %bitcast.114, f32[4096]{0:T(1024)S(1)} %bitcast.125, bf16[5,32,4096]{2,1,0:T(8,128)(2,1)} %param.27, bf16[512,160]{0,1:T(8,128)(2,1)S(1)} %fusion.28), kind=kOutput, calls=%fused_computation.53 | convolution fusion | flops 417366016 | bytes 9289728 | tf_op jit(solution)/shard_map/dot_general | solution.py:154
  230.0 0.3 fusion.20
  230.4 1.9 reshape.355
  232.3 1.8 fusion.77
  234.1 59.4 %all-gather.10.cloned.1.call-done = bf16[4096,512]{1,0:T(8,128)(2,1)} async-done(((bf16[1024,512]{1,0:T(8,128)(2,1)}), bf16[4096,512]{1,0:T(8,128)(2,1)}) %all-gather.10.cloned.1.call-update) | async-done | bytes 4194320 | tf_op jit(solution)/shard_map/all_gather | solution.py:142
  293.4 8.6 %fusion.24 = f32[512,512]{1,0:T(8,128)S(1)} fusion(bf16[4096,512]{1,0:T(8,128)(2,1)} %all-gather.10.cloned.1.call-done, bf16[512,4096]{1,0:T(8,128)(2,1)} %bitcast.108, bf16[512,4096]{1,0:T(8,128)(2,1)} %bitcast.115, f32[4096]{0:T(1024)S(1)} %bitcast.124, bf16[5,32,4096]{2,1,0:T(8,128)(2,1)} %param.27, bf16[512,160]{0,1:T(8,128)(2,1)} %copy-done.25), kind=kOutput, calls=%fused_computation.49 | convolution fusion | flops 2296381440 | bytes 13942784 | tf_op jit(solution)/shard_map/dot_general | solution.py:149
  302.0 1.7 reshape.354
  303.8 1.5 concatenate.10
  305.3 2.2 gather_fusion.5
  307.7 6.3 %exponential_multiply_fusion = (f32[32,16,8,64]{3,2,1,0:T(8,128)}, f32[32,16,8,64]{3,2,1,0:T(8,128)}, f32[32,16,8]{2,1,0:T(8,128)S(1)}, f32[32,16,8,64]{3,2,1,0:T(8,128)}) fusion(f32[32,16,8,64]{3,2,1,0:T(8,128)} %mul.159, f32[32,16,8,64]{3,2,1,0:T(8,128)S(1)} %fusion.77, f32[32,8,64]{2,1,0:T(8,128)S(1)} %get-tuple-element.4, ...), kind=kLoop, calls=%fused_computation.35 | loop fusion | flops 1830912 | bytes 6375936 | tf_op jit(solution)/shard_map/mul | solution.py:81
  314.0 15.2 %multiply_reduce_fusion = f32[32,16,16,8]{3,2,1,0:T(8,128)} fusion(f32[32,16,8,64]{3,2,1,0:T(8,128)S(1)} %fusion.77, f32[32,16,8,64]{3,2,1,0:T(8,128)} %get-tuple-element.10, f32[32,16,8,64]{3,2,1,0:T(8,128)} %mul.159, f32[32,16,8,64]{3,2,1,0:T(8,128)} %reshape.354, pred[16,16]{1,0:T(8,128)(4,1)S(1)} %iota_compare_fusion.3), kind=kLoop, calls=%fused_computation.7 | loop fusion | flops 20905984 | bytes 4456704 | tf_op jit(solution)/shard_map/reduce_sum | solution.py:69
  329.3 4.0 copy.69
  333.3 10.2 %fusion.11 = f32[32,8,16,64]{3,2,1,0:T(8,128)S(1)} fusion(f32[32,8,64,64]{3,2,1,0:T(8,128)} %param.23, f32[32,16,8,64]{3,2,1,0:T(8,128)S(1)} %copy-done.6), kind=kOutput, calls=%fused_computation.33 | convolution fusion | flops 201326592 | bytes 6291456 | tf_op jit(solution)/shard_map/bthi,bhij->bthj/dot_general | solution.py:60
  343.5 3.6 fusion.76
  347.4 1.3 multiply_reduce_fusion.1
  348.9 4.5 copy.82
  353.5 0.7 gather_fusion.6
  354.2 19.7 %multiply_add_fusion = bf16[32,8,64,64]{3,2,1,0:T(8,128)(2,1)} fusion(f32[32,8,64,64]{3,2,1,0:T(8,128)} %param.23, f32[32,8,64]{2,1,0:T(8,128)S(1)} %get-tuple-element.3, f32[32,16,8,64]{3,2,1,0:T(8,128)} %get-tuple-element.7, f32[32,16,8,64]{3,2,1,0:T(8,128)} %reshape.356), kind=kOutput, calls=%fused_computation.23 | convolution fusion | flops 204472320 | bytes 8454144 | tf_op jit(solution)/shard_map/bshi,bshj->bhij/dot_general | solution.py:82
  373.9 7.8 %gather_fusion = bf16[64,8,64,64]{3,2,1,0:T(8,128)(2,1)} fusion(bf16[32,8,64,64]{3,2,1,0:T(8,128)(2,1)} %multiply_add_fusion, s32[1024]{0:T(1024)S(1)} %pad_clamp_fusion.2), kind=kCustom, calls=%fused_computation | custom fusion | bytes 8388864 | tf_op jit(solution)/shard_map/gather | solution.py:218
  381.8 0.7 gather_fusion.3
  382.5 0.7 fusion.56
  383.2 3.5 all-to-all-start.1
  386.7 10.5 %select_convert_fusion = bf16[4,16,8,64,64]{4,3,2,1,0:T(8,128)(2,1)} fusion(bf16[4,16,8,64,64]{4,3,2,1,0:T(8,128)(2,1)} %bitcast.103, pred[4,16]{1,0:T(4,128)(4,1)S(1)} %and_reduce_fusion), kind=kLoop, calls=%fused_computation.15 | loop fusion | flops 2097152 | bytes 8388672 | tf_op jit(solution)/shard_map/convert_element_type | solution.py:225
  397.3 2.2 copy.72
  399.8 0.1 mul.169
  399.9 1.4 copy.79
  401.3 1.5 reshape.357
  403.0 0.3 copy.75
  403.4 9.7 %reshape.439 = bf16[4,2,262144]{2,1,0:T(2,128)(2,1)} reshape(bf16[4,16,8,64,64]{4,3,2,1,0:T(8,128)(2,1)} %select_convert_fusion) | data formatting | bytes 8388608
  413.1 5.1 all-to-all-start
  418.2 0.2 reduce-scatter.2.cloned.1.call-start
  418.5 9.7 %multiply_convert_fusion = bf16[512,512]{1,0:T(8,128)(2,1)} fusion(bf16[4096,512]{1,0:T(8,128)(2,1)} %all-gather.16.cloned.1.call-done, bf16[512,4096]{1,0:T(8,128)(2,1)} %bitcast.109, bf16[512,4096]{1,0:T(8,128)(2,1)} %bitcast.116, f32[4096]{0:T(1024)S(1)} %bitcast.123, f32[512,512]{1,0:T(8,128)S(1)} %copy-done.12, f32[512,512]{1,0:T(8,128)S(1)} %copy-done.11, ...), kind=kOutput, calls=%fused_computation.57 | convolution fusion | flops 2299002880 | bytes 16568320 | tf_op jit(solution)/shard_map/dot_general | solution.py:149
  428.2 67.7 %all-gather.18.cloned.1.call-done = bf16[512,4096]{1,0:T(8,128)(2,1)} async-done(((bf16[512,1024]{1,0:T(8,128)(2,1)}), bf16[512,4096]{1,0:T(8,128)(2,1)}) %all-gather.18.cloned.1.call-update) | async-done | bytes 4194320 | tf_op jit(solution)/shard_map/all_gather | solution.py:180
  495.9 6.7 %convolution_convert_fusion = bf16[512,4096]{1,0:T(8,128)(2,1)} fusion(bf16[512,512]{1,0:T(8,128)(2,1)} %multiply_convert_fusion, bf16[512,4096]{1,0:T(8,128)(2,1)} %all-gather.18.cloned.1.call-done), kind=kOutput, calls=%fused_computation.24 | convolution fusion | flops 2149580800 | bytes 8912896 | tf_op jit(solution)/shard_map/dot_general | solution.py:182
  502.7 0.5 copy-done.23
  503.4 0.2 select_reduce_fusion.1
  503.6 0.7 gather_fusion.1
  504.4 1.2 gather_fusion.4
  505.6 40.1 %all-to-all-done = bf16[4,2,262144]{2,1,0:T(2,128)(2,1)} async-done(((bf16[4,2,262144]{2,1,0:T(2,128)(2,1)}), bf16[4,2,262144]{2,1,0:T(2,128)(2,1)}, u32[]{:S(2)}, u32[]{:S(2)}) %all-to-all-start) | async-done | bytes 4194336 | tf_op jit(solution)/shard_map/all_to_all | solution.py:224
  545.7 9.3 %reshape.440 = bf16[4,16,8,64,64]{4,3,2,1,0:T(8,128)(2,1)} reshape(bf16[4,2,262144]{2,1,0:T(2,128)(2,1)} %all-to-all-done) | data formatting | bytes 8388608
  555.0 11.3 %bitcast_convert_fusion = f32[64,8,64,64]{3,2,1,0:T(8,128)} fusion(bf16[4,16,8,64,64]{4,3,2,1,0:T(8,128)(2,1)} %reshape.440), kind=kLoop, calls=%fused_computation.22 | loop fusion | flops 2097152 | bytes 12582912 | tf_op jit(solution)/shard_map/reshape | solution.py:236
  566.3 10.4 %gather_fusion.2 = f32[32,8,64,64]{3,2,1,0:T(8,128)} fusion(f32[64,8,64,64]{3,2,1,0:T(8,128)} %bitcast_convert_fusion, s32[1024]{0:T(1024)S(1)} %pad_clamp_fusion), kind=kCustom, calls=%fused_computation.2 | custom fusion | bytes 8388736 | tf_op jit(solution)/shard_map/gather | solution.py:236
  576.7 2.1 fusion.34
  (101 shorter events, 2.6 us)
Async XLA Ops:
  7.2 47.9 %copy-start = (bf16[4096,160]{0,1:T(8,128)(2,1)S(1)}, bf16[4096,160]{0,1:T(8,128)(2,1)}, u32[]{:S(2)}) copy-start(bf16[4096,160]{0,1:T(8,128)(2,1)} %param.26) | copy-start | bytes 3932164
  7.2 4.0 copy-start.18
  7.2 4.2 copy-start.24
  7.2 5.0 copy-start.15
  7.2 16.4 %copy-start.14 = (f32[5,4096]{1,0:T(8,128)S(1)}, f32[5,4096]{1,0:T(8,128)}, u32[]{:S(2)}) copy-start(f32[5,4096]{1,0:T(8,128)} %param.25) | copy-start | bytes 245764
  7.2 42.2 %all-gather.8.cloned.1.call-start = ((), (), s32[]{:S(2)}) async-start(), calls=%async_computation.3 | async-start | bytes 4718592 | tf_op jit(solution)/shard_map/all_gather | solution.py:128
  8.0 123.8 %all-gather.12.cloned.1.call-start = ((), (), s32[]{:S(2)}) async-start(), calls=%async_computation.5 | async-start | bytes 5242880 | tf_op jit(solution)/shard_map/all_gather | solution.py:144
  8.7 204.0 %all-gather.14.cloned.1.call-start = ((), (), s32[]{:S(2)}) async-start(), calls=%async_computation.6 | async-start | bytes 5242880 | tf_op jit(solution)/shard_map/all_gather | solution.py:143
  9.4 284.0 %all-gather.10.cloned.1.call-start = ((), (), s32[]{:S(2)}) async-start(), calls=%async_computation.4 | async-start | bytes 5242880 | tf_op jit(solution)/shard_map/all_gather | solution.py:142
  10.0 408.5 %all-gather.16.cloned.1.call-start = ((), (), s32[]{:S(2)}) async-start(), calls=%async_computation.7 | async-start | bytes 5242880 | tf_op jit(solution)/shard_map/all_gather | solution.py:145
  10.6 485.3 %all-gather.18.cloned.1.call-start = ((), (), s32[]{:S(2)}) async-start(), calls=%async_computation.8 | async-start | bytes 5242880 | tf_op jit(solution)/shard_map/all_gather | solution.py:180
  23.1 30.1 %copy-start.8 = (bf16[32,1,4096]{2,0,1:T(8,128)(2,1)}, bf16[32,1,4096]{2,0,1:T(8,128)(2,1)S(1)}, u32[]{:S(2)}) copy-start(bf16[32,1,4096]{2,0,1:T(8,128)(2,1)S(1)} %broadcast_in_dim.75) | copy-start | bytes 786436
  49.4 5.7 copy-start.3
  49.4 5.7 copy-start.20
  53.1 1.9 copy-start.7
  57.1 166.0 %copy-start.25 = (bf16[512,160]{0,1:T(8,128)(2,1)}, bf16[512,160]{0,1:T(8,128)(2,1)S(1)}, u32[]{:S(2)}) copy-start(bf16[512,160]{0,1:T(8,128)(2,1)S(1)} %fusion.28) | copy-start | bytes 491524
  212.7 10.4 %copy-start.19 = (bf16[4096,64]{0,1:T(8,128)(2,1)S(1)}, bf16[4096,64]{0,1:T(8,128)(2,1)}, u32[]{:S(2)}) copy-start(bf16[4096,64]{0,1:T(8,128)(2,1)} %param.29) | copy-start | bytes 1572868
  223.1 6.9 %copy-start.13 = (bf16[64,512]{1,0:T(8,128)(2,1)S(1)}, bf16[64,512]{1,0:T(8,128)(2,1)}, u32[]{:S(2)}) copy-start(bf16[64,512]{1,0:T(8,128)(2,1)} %param.30) | copy-start | bytes 196612
  223.1 6.9 %copy-start.17 = (f32[512]{0:T(512)S(1)}, f32[512]{0:T(512)}, u32[]{:S(2)}) copy-start(f32[512]{0:T(512)} %param.28) | copy-start | bytes 6148
  302.0 5.6 copy-start.16
  329.3 4.0 copy-start.6
  333.3 10.2 %copy-start.2 = (f32[32,16,8,64]{3,2,1,0:T(8,128)S(1)}, f32[32,16,8,64]{3,2,1,0:T(8,128)}, u32[]{:S(2)}) copy-start(f32[32,16,8,64]{3,2,1,0:T(8,128)} %reshape.356) | copy-start | bytes 3145732
  333.3 10.2 %copy-start.5 = (f32[32,16,16,8]{2,1,3,0:T(8,128)S(1)}, f32[32,16,16,8]{2,1,3,0:T(8,128)}, u32[]{:S(2)}) copy-start(f32[32,16,16,8]{2,1,3,0:T(8,128)} %copy.69) | copy-start | bytes 786436
  348.8 4.5 copy-start.9
  383.2 29.9 %all-to-all-start.1 = ((bf16[4,16,512]{2,1,0:T(8,128)(2,1)}), bf16[4,16,512]{2,1,0:T(8,128)(2,1)S(1)}, u32[]{:S(2)}, u32[]{:S(2)}) async-start(bf16[4,16,512]{2,1,0:T(8,128)(2,1)} %fusion.56), calls=%async_computation.2 | async-start | bytes 131072 | tf_op jit(solution)/shard_map/all_to_all | solution.py:227
  399.5 1.9 copy-start.4
  413.1 5.4 copy-start.11
  413.1 5.4 copy-start.12
  413.1 5.5 copy-start.21
  413.1 5.5 copy-start.22
  413.1 132.6 %all-to-all-start = ((bf16[4,2,262144]{2,1,0:T(2,128)(2,1)}), bf16[4,2,262144]{2,1,0:T(2,128)(2,1)}, u32[]{:S(2)}, u32[]{:S(2)}) async-start(bf16[4,2,262144]{2,1,0:T(2,128)(2,1)} %reshape.439), calls=%async_computation.1 | async-start | bytes 8388608 | tf_op jit(solution)/shard_map/all_to_all | solution.py:224
  418.2 158.5 %reduce-scatter.2.cloned.1.call-start = ((), (), s32[]{:S(2)}) async-start(), calls=%async_computation.9 | async-start | bytes 4718592 | tf_op jit(solution)/shard_map/reduce_scatter | solution.py:181
  502.6 0.7 copy-start.23
  566.3 10.4 %copy-start.10 = (bf16[4,16,4096]{2,1,0:T(8,128)(2,1)S(1)}, bf16[4,16,4096]{2,1,0:T(8,128)(2,1)}, u32[]{:S(2)}) copy-start(bf16[4,16,4096]{2,1,0:T(8,128)(2,1)} %param.21) | copy-start | bytes 1572868
  566.3 12.5 %copy-start.1 = (bf16[4096,160]{0,1:T(8,128)(2,1)S(1)}, bf16[4096,160]{0,1:T(8,128)(2,1)}, u32[]{:S(2)}) copy-start(bf16[4096,160]{0,1:T(8,128)(2,1)} %param.26) | copy-start | bytes 3932164
Sparse Core Ops, SparseCore 0:
  9.9 39.4 all-gather.7
  51.0 80.7 all-gather.11
  133.4 79.2 all-gather.13
  214.1 79.2 all-gather.9
  294.9 79.2 all-gather.15
  375.6 120.2 all-gather.17
  502.8 49.4 reduce-scatter.1
where the time goes:
time: 590 us; the launch traced here: 586 us
  waiting for transfers between devices  342 us (58%)
  matrix products  84.8 us (14%)
  local copies, waits for them, and re-layouts  70.2 us (12%)
  other arithmetic  54.3 us (9%)
  between operations  15 us (3%)
  blocking collectives  10.8 us (2%)
  starting transfers between devices  9.1 us (2%)
    all_gather x1, waiting for transfers between devices, on_device(): lax.all_gather(payload_matrix, 'dp', axis=0, tiled=True)  74.7 us
    all_gather x1, waiting for transfers between devices, on_device(): lax.all_gather(lookup_matrix, 'dp', axis=0, tiled=True)  70.5 us
    all_gather x1, waiting for transfers between devices, on_device(): out_cols = lax.all_gather(emission_matrix, 'dp', axis=1, tiled=True)  67.7 us
    all_gather x1, waiting for transfers between devices, on_device(): lax.all_gather(acceptor_matrix, 'dp', axis=0, tiled=True)  59.4 us
    all_to_all x1, waiting for transfers between devices, on_device(): lax.all_to_all(send_state.astype(jnp.bfloat16), 'dp', split_axis=0, conca...  40.1 us
    dot_general x4, matrix products, on_device(): jnp.dot(source_rows, piece, preferred_element_type=jnp.float32)  35.4 us
    all_gather x1, waiting for transfers between devices, on_device(): lax.all_gather(guess_vectors, 'mp', axis=0, tiled=True)  25.6 us
    unnamed x55, local copies, waits for them, and re-layouts  21.5 us
  transfers between devices with their start and end apart: 9, of which 6 were waited for; matrix products, arithmetic and copies ran while one was open for 35% of the time, Pallas kernels for 0%

commit v1 on v0

--- a/solution.py
+++ b/solution.py
@@ -5,6 +5,24 @@
 
 GROUP_DIMENSION = 64
 norm_eps = 0.00064
+
+
+def collect(value, axis, dim):
+    ways, here, step = (lax.axis_size(axis), lax.axis_index(axis), value.shape[dim])
+    shape = [n * ways if d == dim else n for d, n in enumerate(value.shape)]
+    full = lax.dynamic_update_slice_in_dim(
+        jnp.zeros(shape, value.dtype), value, here * step, axis=dim
+    )
+    going_up = going_down = value
+    for far in range(1, ways // 2 + 1):
+        going_up = lax.ppermute(going_up, axis, [(d, (d + 1) % ways) for d in range(ways)])
+        full = lax.dynamic_update_slice_in_dim(full, going_up, (here - far) % ways * step, axis=dim)
+        if 2 * far < ways:
+            going_down = lax.ppermute(going_down, axis, [(d, (d - 1) % ways) for d in range(ways)])
+            full = lax.dynamic_update_slice_in_dim(
+                full, going_down, (here + far) % ways * step, axis=dim
+            )
+    return full
 
 
 def token_mixes(
@@ -140,7 +158,7 @@
     sources = (shift_mixed_rows[3], shift_mixed_rows[1], shift_mixed_rows[2], shift_mixed_rows[4])
     pieces = (
         lax.all_gather(acceptor_matrix, "dp", axis=0, tiled=True),
-        lax.all_gather(lookup_matrix, "dp", axis=0, tiled=True),
+        collect(lookup_matrix, "dp", 0),
         lax.all_gather(payload_matrix, "dp", axis=0, tiled=True),
         lax.all_gather(gating_matrix, "dp", axis=0, tiled=True),
     )

time: 590 us -> 530 us (0.90)
  waiting for transfers between devices: 342 us -> 267 us
  local copies, waits for them, and re-layouts: 70.2 us -> 79.3 us
    all_gather x1 -> x0, waiting for transfers between devices: 70.5 us -> none  [on_device(): lax.all_gather(lookup_matrix, 'dp', axis=0, tiled=True)]
    ppermute x0 -> x3, waiting for transfers between devices: none -> 69.6 us  [the longest x2 50.7 us: collect(): lax.ppermute(going_up, axis, [(d, (d + 1) % ways) for d in range(ways)])]
    all_gather x1, waiting for transfers between devices: 74.7 us -> 37.9 us  [on_device(): lax.all_gather(payload_matrix, 'dp', axis=0, tiled=True)]
    all_gather x1, waiting for transfers between devices: 25.6 us -> 0.01 us  [on_device(): lax.all_gather(guess_vectors, 'mp', axis=0, tiled=True)]
    all_gather x1, waiting for transfers between devices: 59.4 us -> 49.8 us  [on_device(): lax.all_gather(acceptor_matrix, 'dp', axis=0, tiled=True)]
    dynamic_update_slice x0 -> x4, local copies, waits for them, and re-layouts: none -> 6.71 us  [the longest x2 3.31 us: collect(): lax.dynamic_update_slice_in_dim(full, going_up, (here - far) % ways * ste...]
    unnamed x55 -> x59, local copies, waits for them, and re-layouts: 21.5 us -> 21.6 us
  transfers between devices with their start and end apart: 9 -> 11, of which waited for: 6 -> 7; matrix products, arithmetic and copies ran while one was open for 35% -> 41% of each run, Pallas kernels for 0% -> 0%
where the time goes in v1:
time: 530 us; the launch traced here: 526 us
  waiting for transfers between devices  267 us (50%)
  matrix products  84.8 us (16%)
  local copies, waits for them, and re-layouts  79.3 us (15%)
  other arithmetic  54.4 us (10%)
  between operations  14.9 us (3%)
  starting transfers between devices  14.2 us (3%)
  blocking collectives  10.4 us (2%)
    all_gather x1, waiting for transfers between devices, on_device(): out_cols = lax.all_gather(emission_matrix, 'dp', axis=1, tiled=True)  67.2 us
    ppermute x2, waiting for transfers between devices, collect(): lax.ppermute(going_up, axis, [(d, (d + 1) % ways) for d in range(ways)])  50.7 us
    all_gather x1, waiting for transfers between devices, on_device(): lax.all_gather(acceptor_matrix, 'dp', axis=0, tiled=True)  49.8 us
    all_to_all x1, waiting for transfers between devices, on_device(): lax.all_to_all(send_state.astype(jnp.bfloat16), 'dp', split_axis=0, conca...  40.3 us
    all_gather x1, waiting for transfers between devices, on_device(): lax.all_gather(payload_matrix, 'dp', axis=0, tiled=True)  37.9 us
    dot_general x4, matrix products, on_device(): jnp.dot(source_rows, piece, preferred_element_type=jnp.float32)  35.3 us
    unnamed x59, local copies, waits for them, and re-layouts  21.6 us
    dot_general x1, matrix products, wkv_blocks(): jnp.einsum('bshi,bshj->bhij', weighted, payload_vectors, precision=lax.Pr...  19.8 us
  transfers between devices with their start and end apart: 11, of which 7 were waited for; matrix products, arithmetic and copies ran while one was open for 41% of the time, Pallas kernels for 0%

profile of v1, /device:TPU:0, one launch (start us, length us, event | category | flops | bytes accessed | tf_op | source)
XLA Modules:
  0.0 525.5 jit_solution(11967678795542508828)
XLA Ops:
  7.2 0.7 all-gather.7.cloned.1.call-update
  8.0 0.7 all-gather.11.cloned.1.call-update
  8.7 0.7 all-gather.9.cloned.1.call-update
  9.5 0.5 all-gather.13.cloned.1.call-update
  10.1 3.1 collective-permute-start
  13.1 2.1 collective-permute-start.1
  16.4 2.3 broadcast_in_dim.78
  18.6 1.0 constant_dynamic-update-slice_fusion.3
  19.8 10.4 %all-gather = bf16[8,4,4096]{2,1,0:T(4,128)(2,1)S(1)} all-gather(bf16[1,4,4096]{2,1,0:T(4,128)(2,1)S(1)} %bitcast.122), channel_id=1, replica_groups=mesh['dp'=4,'mp'=8] {'mp'}, dimensions={0}, use_global_device_ids=true | all-gather | bytes 294912 | tf_op jit(solution)/shard_map/all_gather | solution.py:147
  30.3 0.5 copy.66
  30.9 8.7 %collective-permute-done = bf16[1024,512]{1,0:T(8,128)(2,1)} collective-permute-done((bf16[1024,512]{1,0:T(8,128)(2,1)}, bf16[1024,512]{1,0:T(8,128)(2,1)}, u32[]{:S(2)}, u32[]{:S(2)}) %collective-permute-start) | collective-permute-done | bytes 1048608 | tf_op jit(solution)/shard_map/ppermute | solution.py:18
  39.6 2.3 constant_dynamic-update-slice_fusion.2
  41.9 18.9 %collective-permute-done.1 = bf16[1024,512]{1,0:T(8,128)(2,1)} collective-permute-done((bf16[1024,512]{1,0:T(8,128)(2,1)}, bf16[1024,512]{1,0:T(8,128)(2,1)}, u32[]{:S(2)}, u32[]{:S(2)}) %collective-permute-start.1) | collective-permute-done | bytes 1048608 | tf_op jit(solution)/shard_map/ppermute | solution.py:21
  60.8 2.4 constant_dynamic-update-slice_fusion.1
  63.1 42.0 %collective-permute-done.2 = bf16[1024,512]{1,0:T(8,128)(2,1)S(1)} collective-permute-done((bf16[1024,512]{1,0:T(8,128)(2,1)}, bf16[1024,512]{1,0:T(8,128)(2,1)S(1)}, u32[]{:S(2)}, u32[]{:S(2)}) %collective-permute-start.2) | collective-permute-done | bytes 1048608 | tf_op jit(solution)/shard_map/ppermute | solution.py:18
  105.1 1.0 constant_dynamic-update-slice_fusion
  106.2 3.6 pad_maximum_fusion
  109.9 1.9 copy-done.7
  111.8 2.0 fusion.28
  113.8 37.9 %all-gather.11.cloned.1.call-done = bf16[4096,512]{1,0:T(8,128)(2,1)} async-done(((bf16[1024,512]{1,0:T(8,128)(2,1)}), bf16[4096,512]{1,0:T(8,128)(2,1)}) %all-gather.11.cloned.1.call-update) | async-done | bytes 4194320 | tf_op jit(solution)/shard_map/all_gather | solution.py:162
  151.7 8.5 %fusion.23 = f32[512,512]{1,0:T(8,128)S(1)} fusion(bf16[4096,512]{1,0:T(8,128)(2,1)} %all-gather.11.cloned.1.call-done, bf16[512,4096]{1,0:T(8,128)(2,1)} %bitcast.105, bf16[512,4096]{1,0:T(8,128)(2,1)} %bitcast.112, f32[4096]{0:T(1024)S(1)} %bitcast.127, bf16[5,32,4096]{2,1,0:T(8,128)(2,1)S(1)} %copy-done.20, bf16[512,160]{0,1:T(8,128)(2,1)S(1)} %fusion.28), kind=kOutput, calls=%fused_computation.48 | convolution fusion | flops 2296381440 | bytes 13942784 | tf_op jit(solution)/shard_map/dot_general | solution.py:167
  160.1 1.8 reshape.356
  161.9 8.6 %fusion.22 = f32[512,512]{1,0:T(8,128)S(1)} fusion(bf16[4096,512]{1,0:T(8,128)(2,1)} %constant_dynamic-update-slice_fusion, bf16[512,4096]{1,0:T(8,128)(2,1)} %bitcast.106, bf16[512,4096]{1,0:T(8,128)(2,1)} %bitcast.113, f32[4096]{0:T(1024)S(1)} %bitcast.126, bf16[5,32,4096]{2,1,0:T(8,128)(2,1)S(1)} %copy-done.20, bf16[512,160]{0,1:T(8,128)(2,1)} %copy-done.27), kind=kOutput, calls=%fused_computation.47 | convolution fusion | flops 2296381440 | bytes 13942784 | tf_op jit(solution)/shard_map/dot_general | solution.py:167
  170.5 1.8 mul.175
  172.4 6.9 %fusion.32 = bf16[512,64]{0,1:T(8,128)(2,1)S(1)} fusion(bf16[4096,64]{0,1:T(8,128)(2,1)S(1)} %copy-done.21, bf16[512,4096]{1,0:T(8,128)(2,1)} %bitcast.107, bf16[512,4096]{1,0:T(8,128)(2,1)} %bitcast.114, f32[4096]{0:T(1024)S(1)} %bitcast.125, bf16[5,32,4096]{2,1,0:T(8,128)(2,1)S(1)} %copy-done.20, bf16[512,160]{0,1:T(8,128)(2,1)} %copy-done.27), kind=kOutput, calls=%fused_computation.53 | convolution fusion | flops 417366016 | bytes 9289728 | tf_op jit(solution)/shard_map/dot_general | solution.py:172
  179.3 0.3 fusion.20
  179.6 1.9 reshape.355
  181.6 1.7 fusion.77
  183.3 49.8 %all-gather.9.cloned.1.call-done = bf16[4096,512]{1,0:T(8,128)(2,1)} async-done(((bf16[1024,512]{1,0:T(8,128)(2,1)}), bf16[4096,512]{1,0:T(8,128)(2,1)}) %all-gather.9.cloned.1.call-update) | async-done | bytes 4194320 | tf_op jit(solution)/shard_map/all_gather | solution.py:160
  233.1 8.6 %fusion.24 = f32[512,512]{1,0:T(8,128)S(1)} fusion(bf16[4096,512]{1,0:T(8,128)(2,1)} %all-gather.9.cloned.1.call-done, bf16[512,4096]{1,0:T(8,128)(2,1)} %bitcast.108, bf16[512,4096]{1,0:T(8,128)(2,1)} %bitcast.115, f32[4096]{0:T(1024)S(1)} %bitcast.124, bf16[5,32,4096]{2,1,0:T(8,128)(2,1)} %param.27, bf16[512,160]{0,1:T(8,128)(2,1)} %copy-done.27), kind=kOutput, calls=%fused_computation.49 | convolution fusion | flops 2296381440 | bytes 13942784 | tf_op jit(solution)/shard_map/dot_general | solution.py:167
  241.6 1.8 reshape.354
  243.4 1.5 concatenate.10
  245.0 2.2 gather_fusion.5
  247.3 6.3 %exponential_multiply_fusion = (f32[32,16,8,64]{3,2,1,0:T(8,128)}, f32[32,16,8,64]{3,2,1,0:T(8,128)}, f32[32,16,8]{2,1,0:T(8,128)S(1)}, f32[32,16,8,64]{3,2,1,0:T(8,128)}) fusion(f32[32,16,8,64]{3,2,1,0:T(8,128)} %mul.175, f32[32,16,8,64]{3,2,1,0:T(8,128)S(1)} %fusion.77, f32[32,8,64]{2,1,0:T(8,128)S(1)} %get-tuple-element.4, ...), kind=kLoop, calls=%fused_computation.35 | loop fusion | flops 1830912 | bytes 6375936 | tf_op jit(solution)/shard_map/mul | solution.py:99
  253.8 15.2 %multiply_reduce_fusion = f32[32,16,16,8]{3,2,1,0:T(8,128)} fusion(f32[32,16,8,64]{3,2,1,0:T(8,128)S(1)} %fusion.77, f32[32,16,8,64]{3,2,1,0:T(8,128)} %get-tuple-element.10, f32[32,16,8,64]{3,2,1,0:T(8,128)} %mul.175, f32[32,16,8,64]{3,2,1,0:T(8,128)} %reshape.354, pred[16,16]{1,0:T(8,128)(4,1)S(1)} %iota_compare_fusion.3), kind=kLoop, calls=%fused_computation.7 | loop fusion | flops 20905984 | bytes 4456704 | tf_op jit(solution)/shard_map/reduce_sum | solution.py:87
  269.0 4.1 copy.69
  273.1 10.2 %fusion.11 = f32[32,8,16,64]{3,2,1,0:T(8,128)S(1)} fusion(f32[32,8,64,64]{3,2,1,0:T(8,128)} %param.23, f32[32,16,8,64]{3,2,1,0:T(8,128)S(1)} %copy-done.6), kind=kOutput, calls=%fused_computation.33 | convolution fusion | flops 201326592 | bytes 6291456 | tf_op jit(solution)/shard_map/bthi,bhij->bthj/dot_general | solution.py:78
  283.3 3.6 fusion.76
  287.2 1.3 multiply_reduce_fusion.1
  288.7 4.5 copy.82
  293.3 0.7 gather_fusion.6
  294.0 19.8 %multiply_add_fusion = bf16[32,8,64,64]{3,2,1,0:T(8,128)(2,1)} fusion(f32[32,8,64,64]{3,2,1,0:T(8,128)} %param.23, f32[32,8,64]{2,1,0:T(8,128)S(1)} %get-tuple-element.3, f32[32,16,8,64]{3,2,1,0:T(8,128)} %get-tuple-element.7, f32[32,16,8,64]{3,2,1,0:T(8,128)} %reshape.356), kind=kOutput, calls=%fused_computation.23 | convolution fusion | flops 204472320 | bytes 8454144 | tf_op jit(solution)/shard_map/bshi,bshj->bhij/dot_general | solution.py:100
  313.8 7.8 %gather_fusion = bf16[64,8,64,64]{3,2,1,0:T(8,128)(2,1)} fusion(bf16[32,8,64,64]{3,2,1,0:T(8,128)(2,1)} %multiply_add_fusion, s32[1024]{0:T(1024)S(1)} %pad_clamp_fusion.2), kind=kCustom, calls=%fused_computation | custom fusion | bytes 8388864 | tf_op jit(solution)/shard_map/gather | solution.py:236
  321.7 0.7 gather_fusion.3
  322.4 0.7 fusion.56
  323.1 3.5 all-to-all-start.1
  326.6 10.6 %select_convert_fusion = bf16[4,16,8,64,64]{4,3,2,1,0:T(8,128)(2,1)} fusion(bf16[4,16,8,64,64]{4,3,2,1,0:T(8,128)(2,1)} %bitcast.103, pred[4,16]{1,0:T(4,128)(4,1)S(1)} %and_reduce_fusion), kind=kLoop, calls=%fused_computation.15 | loop fusion | flops 2097152 | bytes 8388672 | tf_op jit(solution)/shard_map/convert_element_type | solution.py:243
  337.2 2.2 copy.72
  339.9 1.4 copy.79
  341.2 1.5 reshape.357
  342.9 0.3 copy.75
  343.3 9.7 %reshape.439 = bf16[4,2,262144]{2,1,0:T(2,128)(2,1)} reshape(bf16[4,16,8,64,64]{4,3,2,1,0:T(8,128)(2,1)} %select_convert_fusion) | data formatting | bytes 8388608
  353.0 5.1 all-to-all-start
  358.4 9.7 %multiply_convert_fusion = bf16[512,512]{1,0:T(8,128)(2,1)} fusion(bf16[4096,512]{1,0:T(8,128)(2,1)} %all-gather.13.cloned.1.call-done, bf16[512,4096]{1,0:T(8,128)(2,1)} %bitcast.109, bf16[512,4096]{1,0:T(8,128)(2,1)} %bitcast.116, f32[4096]{0:T(1024)S(1)} %bitcast.123, f32[512,512]{1,0:T(8,128)S(1)} %copy-done.13, f32[512,512]{1,0:T(8,128)S(1)} %copy-done.11, ...), kind=kOutput, calls=%fused_computation.57 | convolution fusion | flops 2299002880 | bytes 16568320 | tf_op jit(solution)/shard_map/dot_general | solution.py:167
  368.1 67.2 %all-gather.15.cloned.1.call-done = bf16[512,4096]{1,0:T(8,128)(2,1)} async-done(((bf16[512,1024]{1,0:T(8,128)(2,1)}), bf16[512,4096]{1,0:T(8,128)(2,1)}) %all-gather.15.cloned.1.call-update) | async-done | bytes 4194320 | tf_op jit(solution)/shard_map/all_gather | solution.py:198
  435.4 6.6 %convolution_convert_fusion = bf16[512,4096]{1,0:T(8,128)(2,1)} fusion(bf16[512,512]{1,0:T(8,128)(2,1)} %multiply_convert_fusion, bf16[512,4096]{1,0:T(8,128)(2,1)} %all-gather.15.cloned.1.call-done), kind=kOutput, calls=%fused_computation.24 | convolution fusion | flops 2149580800 | bytes 8912896 | tf_op jit(solution)/shard_map/dot_general | solution.py:200
  442.1 0.5 copy-done.25
  442.9 0.7 gather_fusion.1
  443.8 1.2 gather_fusion.4
  445.0 40.3 %all-to-all-done = bf16[4,2,262144]{2,1,0:T(2,128)(2,1)} async-done(((bf16[4,2,262144]{2,1,0:T(2,128)(2,1)}), bf16[4,2,262144]{2,1,0:T(2,128)(2,1)}, u32[]{:S(2)}, u32[]{:S(2)}) %all-to-all-start) | async-done | bytes 4194336 | tf_op jit(solution)/shard_map/all_to_all | solution.py:242
  485.3 9.3 %reshape.440 = bf16[4,16,8,64,64]{4,3,2,1,0:T(8,128)(2,1)} reshape(bf16[4,2,262144]{2,1,0:T(2,128)(2,1)} %all-to-all-done) | data formatting | bytes 8388608
  494.6 11.3 %bitcast_convert_fusion = f32[64,8,64,64]{3,2,1,0:T(8,128)} fusion(bf16[4,16,8,64,64]{4,3,2,1,0:T(8,128)(2,1)} %reshape.440), kind=kLoop, calls=%fused_computation.22 | loop fusion | flops 2097152 | bytes 12582912 | tf_op jit(solution)/shard_map/reshape | solution.py:254
  506.0 10.4 %gather_fusion.2 = f32[32,8,64,64]{3,2,1,0:T(8,128)} fusion(f32[64,8,64,64]{3,2,1,0:T(8,128)} %bitcast_convert_fusion, s32[1024]{0:T(1024)S(1)} %pad_clamp_fusion), kind=kCustom, calls=%fused_computation.2 | custom fusion | bytes 8388736 | tf_op jit(solution)/shard_map/gather | solution.py:254
  516.4 2.1 fusion.34
  (113 shorter events, 3.6 us)
Async XLA Ops:
  7.2 104.6 %copy-start = (bf16[4096,160]{0,1:T(8,128)(2,1)S(1)}, bf16[4096,160]{0,1:T(8,128)(2,1)}, u32[]{:S(2)}) copy-start(bf16[4096,160]{0,1:T(8,128)(2,1)} %param.26) | copy-start | bytes 3932164
  7.2 8.1 %copy-start.19 = (s32[128]{0:T(128)S(1)}, s32[128]{0:T(128)}, u32[]{:S(2)}) copy-start(s32[128]{0:T(128)} %param.40) | copy-start | bytes 1540
  7.2 8.2 %copy-start.26 = (s32[128]{0:T(128)S(1)}, s32[128]{0:T(128)}, u32[]{:S(2)}) copy-start(s32[128]{0:T(128)} %param.41) | copy-start | bytes 1540
  7.2 99.0 %all-gather.7.cloned.1.call-start = ((), (), s32[]{:S(2)}) async-start(), calls=%async_computation.3 | async-start | bytes 4718592 | tf_op jit(solution)/shard_map/all_gather | solution.py:146
  7.9 10.7 %copy-start.12 = (bf16[1024,512]{1,0:T(8,128)(2,1)S(1)}, bf16[1024,512]{1,0:T(8,128)(2,1)}, u32[]{:S(2)}) copy-start(bf16[1024,512]{1,0:T(8,128)(2,1)} %param.33) | copy-start | bytes 3145732
  7.9 143.7 %all-gather.11.cloned.1.call-start = ((), (), s32[]{:S(2)}) async-start(), calls=%async_computation.5 | async-start | bytes 5242880 | tf_op jit(solution)/shard_map/all_gather | solution.py:162
  8.7 224.4 %all-gather.9.cloned.1.call-start = ((), (), s32[]{:S(2)}) async-start(), calls=%async_computation.4 | async-start | bytes 5242880 | tf_op jit(solution)/shard_map/all_gather | solution.py:160
  9.4 10.3 %copy-start.16 = (bf16[4,4096]{1,0:T(4,128)(2,1)S(1)}, bf16[4,4096]{1,0:T(4,128)(2,1)}, u32[]{:S(2)}) copy-start(bf16[4,4096]{1,0:T(4,128)(2,1)} %param.22) | copy-start | bytes 98308
  9.4 349.0 %all-gather.13.cloned.1.call-start = ((), (), s32[]{:S(2)}) async-start(), calls=%async_computation.6 | async-start | bytes 5242880 | tf_op jit(solution)/shard_map/all_gather | solution.py:163
  10.0 425.4 %all-gather.15.cloned.1.call-start = ((), (), s32[]{:S(2)}) async-start(), calls=%async_computation.7 | async-start | bytes 5242880 | tf_op jit(solution)/shard_map/all_gather | solution.py:198
  10.1 29.5 %collective-permute-start = (bf16[1024,512]{1,0:T(8,128)(2,1)}, bf16[1024,512]{1,0:T(8,128)(2,1)}, u32[]{:S(2)}, u32[]{:S(2)}) collective-permute-start(bf16[1024,512]{1,0:T(8,128)(2,1)} %param.33), channel_id=1, source_target_pairs={{0,8},{8,16},{16,24},{24,0},{1,9},{9,17},{17,25},{25,1},{2,10},{10... | collective-permute-start | bytes 3145736 | tf_op jit(solution)/shard_map/ppermute | solution.py:18
  13.1 47.6 %collective-permute-start.1 = (bf16[1024,512]{1,0:T(8,128)(2,1)}, bf16[1024,512]{1,0:T(8,128)(2,1)}, u32[]{:S(2)}, u32[]{:S(2)}) collective-permute-start(bf16[1024,512]{1,0:T(8,128)(2,1)} %param.33), channel_id=1, source_target_pairs={{0,24},{8,0},{16,8},{24,16},{1,25},{9,1},{17,9},{25,17},{2,26},{10... | collective-permute-start | bytes 3145736 | tf_op jit(solution)/shard_map/ppermute | solution.py:21
  15.3 24.3 %copy-start.15 = (f32[5,4096]{1,0:T(8,128)S(1)}, f32[5,4096]{1,0:T(8,128)}, u32[]{:S(2)}) copy-start(f32[5,4096]{1,0:T(8,128)} %param.25) | copy-start | bytes 245764
  30.3 79.6 %copy-start.8 = (bf16[32,1,4096]{2,0,1:T(8,128)(2,1)}, bf16[32,1,4096]{2,0,1:T(8,128)(2,1)S(1)}, u32[]{:S(2)}) copy-start(bf16[32,1,4096]{2,0,1:T(8,128)(2,1)S(1)} %broadcast_in_dim.77) | copy-start | bytes 786436
  39.5 65.6 %collective-permute-start.2 = (bf16[1024,512]{1,0:T(8,128)(2,1)}, bf16[1024,512]{1,0:T(8,128)(2,1)S(1)}, u32[]{:S(2)}, u32[]{:S(2)}) collective-permute-start(bf16[1024,512]{1,0:T(8,128)(2,1)} %collective-permute-done), channel_id=1, source_target_pairs={{0,8},{8,16},{16,24},{24,0},{1,9},{9,17},{17,25},{25,1},{2,10},{10... | collective-permute-start | bytes 3145736 | tf_op jit(solution)/shard_map/ppermute | solution.py:18
  106.2 5.6 %copy-start.3 = (bf16[32,16,4096]{2,1,0:T(8,128)(2,1)S(1)}, bf16[32,16,4096]{2,1,0:T(8,128)(2,1)}, u32[]{:S(2)}) copy-start(bf16[32,16,4096]{2,1,0:T(8,128)(2,1)} %all-gather.7.cloned.1.call-done) | copy-start | bytes 12582916
  106.2 5.6 %copy-start.22 = (f32[4096]{0:T(1024)S(1)}, f32[4096]{0:T(1024)}, u32[]{:S(2)}) copy-start(f32[4096]{0:T(1024)} %param.24) | copy-start | bytes 49156
  109.8 1.9 copy-start.7
  111.8 39.9 %copy-start.20 = (bf16[5,32,4096]{2,1,0:T(8,128)(2,1)S(1)}, bf16[5,32,4096]{2,1,0:T(8,128)(2,1)}, u32[]{:S(2)}) copy-start(bf16[5,32,4096]{2,1,0:T(8,128)(2,1)} %param.27) | copy-start | bytes 3932164
  113.8 46.3 %copy-start.27 = (bf16[512,160]{0,1:T(8,128)(2,1)}, bf16[512,160]{0,1:T(8,128)(2,1)S(1)}, u32[]{:S(2)}) copy-start(bf16[512,160]{0,1:T(8,128)(2,1)S(1)} %fusion.28) | copy-start | bytes 491524
  161.9 10.5 %copy-start.21 = (bf16[4096,64]{0,1:T(8,128)(2,1)S(1)}, bf16[4096,64]{0,1:T(8,128)(2,1)}, u32[]{:S(2)}) copy-start(bf16[4096,64]{0,1:T(8,128)(2,1)} %param.29) | copy-start | bytes 1572868
  172.3 6.9 %copy-start.14 = (bf16[64,512]{1,0:T(8,128)(2,1)S(1)}, bf16[64,512]{1,0:T(8,128)(2,1)}, u32[]{:S(2)}) copy-start(bf16[64,512]{1,0:T(8,128)(2,1)} %param.30) | copy-start | bytes 196612
  172.3 6.9 %copy-start.18 = (f32[512]{0:T(512)S(1)}, f32[512]{0:T(512)}, u32[]{:S(2)}) copy-start(f32[512]{0:T(512)} %param.28) | copy-start | bytes 6148
  241.6 5.7 %copy-start.17 = (f32[8,64]{1,0:T(8,128)S(1)}, f32[8,64]{1,0:T(8,128)}, u32[]{:S(2)}) copy-start(f32[8,64]{1,0:T(8,128)} %param.31) | copy-start | bytes 6148
  269.0 4.1 copy-start.6
  273.1 10.2 %copy-start.2 = (f32[32,16,8,64]{3,2,1,0:T(8,128)S(1)}, f32[32,16,8,64]{3,2,1,0:T(8,128)}, u32[]{:S(2)}) copy-start(f32[32,16,8,64]{3,2,1,0:T(8,128)} %reshape.356) | copy-start | bytes 3145732
  273.1 10.2 %copy-start.5 = (f32[32,16,16,8]{2,1,3,0:T(8,128)S(1)}, f32[32,16,16,8]{2,1,3,0:T(8,128)}, u32[]{:S(2)}) copy-start(f32[32,16,16,8]{2,1,3,0:T(8,128)} %copy.69) | copy-start | bytes 786436
  288.7 4.5 copy-start.9
  323.1 29.9 %all-to-all-start.1 = ((bf16[4,16,512]{2,1,0:T(8,128)(2,1)}), bf16[4,16,512]{2,1,0:T(8,128)(2,1)S(1)}, u32[]{:S(2)}, u32[]{:S(2)}) async-start(bf16[4,16,512]{2,1,0:T(8,128)(2,1)} %fusion.56), calls=%async_computation.2 | async-start | bytes 131072 | tf_op jit(solution)/shard_map/all_to_all | solution.py:245
  339.4 1.8 copy-start.4
  353.0 5.4 %copy-start.11 = (f32[512,512]{1,0:T(8,128)S(1)}, f32[512,512]{1,0:T(8,128)}, u32[]{:S(2)}) copy-start(f32[512,512]{1,0:T(8,128)} %reshape.357) | copy-start | bytes 3145732
  353.0 5.4 %copy-start.13 = (f32[512,512]{1,0:T(8,128)S(1)}, f32[512,512]{1,0:T(8,128)}, u32[]{:S(2)}) copy-start(f32[512,512]{1,0:T(8,128)} %copy.79) | copy-start | bytes 3145732
  353.0 5.4 %copy-start.23 = (f32[512]{0:T(512)S(1)}, f32[512]{0:T(512)}, u32[]{:S(2)}) copy-start(f32[512]{0:T(512)} %param.38) | copy-start | bytes 6148
  353.0 5.5 %copy-start.24 = (f32[512]{0:T(512)S(1)}, f32[512]{0:T(512)}, u32[]{:S(2)}) copy-start(f32[512]{0:T(512)} %param.37) | copy-start | bytes 6148
  353.0 132.3 %all-to-all-start = ((bf16[4,2,262144]{2,1,0:T(2,128)(2,1)}), bf16[4,2,262144]{2,1,0:T(2,128)(2,1)}, u32[]{:S(2)}, u32[]{:S(2)}) async-start(bf16[4,2,262144]{2,1,0:T(2,128)(2,1)} %reshape.439), calls=%async_computation.1 | async-start | bytes 8388608 | tf_op jit(solution)/shard_map/all_to_all | solution.py:242
  358.1 158.2 %reduce-scatter.2.cloned.1.call-start = ((), (), s32[]{:S(2)}) async-start(), calls=%async_computation.8 | async-start | bytes 4718592 | tf_op jit(solution)/shard_map/reduce_scatter | solution.py:199
  442.0 0.7 copy-start.25
  506.0 10.4 %copy-start.10 = (bf16[4,16,4096]{2,1,0:T(8,128)(2,1)S(1)}, bf16[4,16,4096]{2,1,0:T(8,128)(2,1)}, u32[]{:S(2)}) copy-start(bf16[4,16,4096]{2,1,0:T(8,128)(2,1)} %param.21) | copy-start | bytes 1572868
  506.0 12.5 %copy-start.1 = (bf16[4096,160]{0,1:T(8,128)(2,1)S(1)}, bf16[4096,160]{0,1:T(8,128)(2,1)}, u32[]{:S(2)}) copy-start(bf16[4096,160]{0,1:T(8,128)(2,1)} %param.26) | copy-start | bytes 3932164
Sparse Core Ops, SparseCore 0:
  9.9 40.2 all-gather.6
  51.8 99.7 all-gather.10
  153.2 79.7 all-gather.8
  234.5 79.2 all-gather.12
  315.2 120.1 all-gather.14
  442.2 49.4 reduce-scatter.1
